TPU v7x, 32 devices: a whole 2x2x4 slice. The times are simulated.
32 devices in a mesh: blk: 16 (over z, y, core), split: 2 (over x).
Axes of the slice: x: 2, y: 2, z: 4, core: 2. Of those that a mesh axis runs over, the one named last changes fastest.
Arguments:
- user_factors: float32 [8192, 512], P(('blk', 'split')), may hold values from -2 to 2
- item_factors: float32 [2048, 512], P('blk'), may hold values from -2 to 2
- obs_items: int32 [8192, 4, 8], P(('blk', 'split')), may hold values from 0 to 127
- obs_conf: int32 [8192, 4, 8], P(('blk', 'split')), may hold values from 1 to 3
Outputs:
- users_out: float32 [8192, 512], P(('blk', 'split'))
- items_out: float32 [2048, 512], P(('blk', 'split'))
All inputs are finite; a program needn't handle non-finite values.
Results may differ from a plain program's by a relative error of at most 0.0003.
Values sent between devices are 32-bit elements; how exact they have to be, the bound alone decides.
A program may use at most 64 MiB of HBM per device.

v0:
```python
import jax
import jax.numpy as jnp
from jax import lax
from jax.sharding import PartitionSpec as P

SUBS = 4


LEARN_RATE = 0.0005
CONF_SCALE = 0.5
RIDGE_COEF = 0.01


def passed_along(block, axis, distance):
    devices = range(lax.axis_size(axis))
    route = [((i - distance) % len(devices), i) for i in devices]
    return lax.ppermute(block, axis, route)


def dense_counts(obs_rows, conf_rows, slab_rows):
    columns = lax.broadcasted_iota(jnp.int32, (1, 1, slab_rows), 2)
    hits = jnp.where(
        obs_rows[:, :, None] == columns, conf_rows[:, :, None].astype(jnp.float32), jnp.float32(0.0)
    )
    return jnp.sum(hits, axis=1)


def block_step(user_rows, held, counts):
    scores = lax.dot_general(
        user_rows,
        held,
        (((1,), (1,)), ((), ())),
        precision=lax.Precision.HIGHEST,
        preferred_element_type=jnp.float32,
    )
    target = jnp.where(counts > 0, 1.0, 0.0).astype(jnp.float32)
    weights = 1.0 + CONF_SCALE * counts
    errors = weights * (scores - target)
    grad_user = (
        jnp.dot(errors, held, precision=lax.Precision.HIGHEST, preferred_element_type=jnp.float32)
        + RIDGE_COEF * user_rows
    )
    partial_grad = lax.dot_general(
        errors,
        user_rows,
        (((0,), (0,)), ((), ())),
        precision=lax.Precision.HIGHEST,
        preferred_element_type=jnp.float32,
    )
    return (user_rows - LEARN_RATE * grad_user, partial_grad)


def local(user_factors, item_factors, obs_items, obs_conf):
    slab_rows = item_factors.shape[0]
    share_rows = slab_rows // lax.axis_size("split")
    share_start = lax.axis_index("split") * share_rows
    user_rows = user_factors
    held = item_factors
    for step in range(SUBS):
        counts = dense_counts(obs_items[:, step, :], obs_conf[:, step, :], slab_rows)
        user_rows, partial_grad = block_step(user_rows, held, counts)
        total_grad = lax.psum(partial_grad, "split")
        held = held - LEARN_RATE * (total_grad + RIDGE_COEF * held)
        held = passed_along(held, "blk", -1)
    share_out = lax.dynamic_slice_in_dim(held, share_start, share_rows, 0)
    return (user_rows, share_out)


def solution(mesh):
    in_specs = (
        P(("blk", "split"), None),
        P("blk", None),
        P(("blk", "split"), None, None),
        P(("blk", "split"), None, None),
    )
    out_specs = (P(("blk", "split"), None), P(("blk", "split"), None))
    return jax.shard_map(local, mesh=mesh, in_specs=in_specs, out_specs=out_specs, check_vma=False)
```

profile of v0, /device:TPU:1, one launch (start us, length us, event | category | flops | bytes accessed | tf_op | source)
XLA Modules:
  0.0 152.7 jit_solution(5387052052408175737)
XLA Ops:
  7.2 0.0 all-reduce.5.cloned.1.call-start
  7.2 0.8 slice_bitcast_fusion
  8.0 0.1 copy.14
  8.1 0.8 convert_bitcast_fusion
  8.9 0.1 copy.15
  9.0 1.3 select_reduce_fusion.3
  10.3 0.6 fusion.11
  10.9 1.2 fusion.12
  12.1 0.0 all-reduce.5.cloned.1.call-update
  12.1 0.0 all-reduce.7.cloned.1.call-start
  12.1 0.1 copy.16
  12.3 0.1 copy.17
  12.4 24.7 %all-reduce.5.cloned.1.call-done = f32[128,512]{1,0:T(8,128)} async-done(((f32[128,512]{1,0:T(8,128)}), f32[128,512]{1,0:T(8,128)}) %all-reduce.5.cloned.1.call-update) | async-done | bytes 262160 | tf_op jit(solution)/shard_map/psum | solution.py:62
  37.1 1.0 multiply_subtract_fusion.3
  38.1 1.2 collective-permute-start
  39.3 1.2 select_reduce_fusion.2
  40.5 0.7 fusion.7
  41.2 3.2 %collective-permute-done = f32[128,512]{1,0:T(8,128)S(1)} collective-permute-done((f32[128,512]{1,0:T(8,128)S(1)}, f32[128,512]{1,0:T(8,128)S(1)}, u32[]{:S(2)}, u32[]{:S(2)}) %collective-permute-start) | collective-permute-done | bytes 262176 | tf_op jit(solution)/shard_map/ppermute | solution.py:17
  44.4 0.6 fusion.10
  45.0 1.2 fusion.13
  46.2 0.0 all-reduce.9.cloned.1.call-start
  46.2 0.1 copy.18
  46.3 0.1 copy.19
  46.5 24.3 %all-reduce.7.cloned.1.call-done = f32[128,512]{1,0:T(8,128)} async-done(((f32[128,512]{1,0:T(8,128)}), f32[128,512]{1,0:T(8,128)}) %all-reduce.7.cloned.1.call-update) | async-done | bytes 262160 | tf_op jit(solution)/shard_map/psum | solution.py:62
  70.8 1.0 multiply_subtract_fusion.2
  71.8 1.2 collective-permute-start.1
  73.0 1.2 select_reduce_fusion.1
  74.2 0.7 fusion.5
  74.9 3.2 %collective-permute-done.1 = f32[128,512]{1,0:T(8,128)S(1)} collective-permute-done((f32[128,512]{1,0:T(8,128)S(1)}, f32[128,512]{1,0:T(8,128)S(1)}, u32[]{:S(2)}, u32[]{:S(2)}) %collective-permute-start.1) | collective-permute-done | bytes 262176 | tf_op jit(solution)/shard_map/ppermute | solution.py:17
  78.1 0.6 fusion.9
  78.7 1.2 fusion.14
  79.9 0.0 all-reduce.11.cloned.1.call-start
  79.9 0.1 copy.20
  80.0 0.1 copy.21
  80.2 24.3 %all-reduce.9.cloned.1.call-done = f32[128,512]{1,0:T(8,128)} async-done(((f32[128,512]{1,0:T(8,128)}), f32[128,512]{1,0:T(8,128)}) %all-reduce.9.cloned.1.call-update) | async-done | bytes 262160 | tf_op jit(solution)/shard_map/psum | solution.py:62
  104.5 1.0 multiply_subtract_fusion.1
  105.5 1.2 collective-permute-start.2
  106.7 1.2 select_reduce_fusion
  107.9 0.7 fusion.3
  108.6 3.2 %collective-permute-done.2 = f32[128,512]{1,0:T(8,128)S(1)} collective-permute-done((f32[128,512]{1,0:T(8,128)S(1)}, f32[128,512]{1,0:T(8,128)S(1)}, u32[]{:S(2)}, u32[]{:S(2)}) %collective-permute-start.2) | collective-permute-done | bytes 262176 | tf_op jit(solution)/shard_map/ppermute | solution.py:17
  111.8 0.6 fusion.8
  112.4 1.2 fusion.15
  113.6 24.6 %all-reduce.11.cloned.1.call-done = f32[128,512]{1,0:T(8,128)} async-done(((f32[128,512]{1,0:T(8,128)}), f32[128,512]{1,0:T(8,128)}) %all-reduce.11.cloned.1.call-update) | async-done | bytes 262160 | tf_op jit(solution)/shard_map/psum | solution.py:62
  138.2 1.0 multiply_subtract_fusion
  139.2 1.2 collective-permute-start.3
  140.3 1.4 fusion.1
  141.8 3.7 %collective-permute-done.3 = f32[128,512]{1,0:T(8,128)S(1)} collective-permute-done((f32[128,512]{1,0:T(8,128)S(1)}, f32[128,512]{1,0:T(8,128)S(1)}, u32[]{:S(2)}, u32[]{:S(2)}) %collective-permute-start.3) | collective-permute-done | bytes 262176 | tf_op jit(solution)/shard_map/ppermute | solution.py:17
  145.5 0.7 constant_dynamic-slice_fusion
  (7 shorter events, 0.1 us)
Async XLA Ops:
  7.2 3.1 %copy-start = (f32[256,512]{1,0:T(8,128)S(1)}, f32[256,512]{1,0:T(8,128)}, u32[]{:S(2)}) copy-start(f32[256,512]{1,0:T(8,128)} %param.4) | copy-start | bytes 1572868
  7.2 29.9 %all-reduce.5.cloned.1.call-start = ((), (), s32[]{:S(2)}) async-start(), calls=%async_computation | async-start | bytes 524288 | tf_op jit(solution)/shard_map/psum | solution.py:62
  8.9 1.4 copy-start.1
  12.1 58.7 %all-reduce.7.cloned.1.call-start = ((), (), s32[]{:S(2)}) async-start(), calls=%async_computation.1 | async-start | bytes 524288 | tf_op jit(solution)/shard_map/psum | solution.py:62
  38.1 6.3 %collective-permute-start = (f32[128,512]{1,0:T(8,128)S(1)}, f32[128,512]{1,0:T(8,128)S(1)}, u32[]{:S(2)}, u32[]{:S(2)}) collective-permute-start(f32[128,512]{1,0:T(8,128)S(1)} %multiply_subtract_fusion.3), channel_id=1, source_target_pairs={{2,0},{4,2},{6,4},{8,6},{10,8},{12,10},{14,12},{16,14},{18,16},{20... | collective-permute-start | bytes 786440 | tf_op jit(solution)/shard_map/ppermute | solution.py:17
  46.2 58.3 %all-reduce.9.cloned.1.call-start = ((), (), s32[]{:S(2)}) async-start(), calls=%async_computation.2 | async-start | bytes 524288 | tf_op jit(solution)/shard_map/psum | solution.py:62
  71.8 6.3 %collective-permute-start.1 = (f32[128,512]{1,0:T(8,128)S(1)}, f32[128,512]{1,0:T(8,128)S(1)}, u32[]{:S(2)}, u32[]{:S(2)}) collective-permute-start(f32[128,512]{1,0:T(8,128)S(1)} %multiply_subtract_fusion.2), channel_id=1, source_target_pairs={{2,0},{4,2},{6,4},{8,6},{10,8},{12,10},{14,12},{16,14},{18,16},{20... | collective-permute-start | bytes 786440 | tf_op jit(solution)/shard_map/ppermute | solution.py:17
  79.9 58.3 %all-reduce.11.cloned.1.call-start = ((), (), s32[]{:S(2)}) async-start(), calls=%async_computation.3 | async-start | bytes 524288 | tf_op jit(solution)/shard_map/psum | solution.py:62
  105.5 6.3 %collective-permute-start.2 = (f32[128,512]{1,0:T(8,128)S(1)}, f32[128,512]{1,0:T(8,128)S(1)}, u32[]{:S(2)}, u32[]{:S(2)}) collective-permute-start(f32[128,512]{1,0:T(8,128)S(1)} %multiply_subtract_fusion.1), channel_id=1, source_target_pairs={{2,0},{4,2},{6,4},{8,6},{10,8},{12,10},{14,12},{16,14},{18,16},{20... | collective-permute-start | bytes 786440 | tf_op jit(solution)/shard_map/ppermute | solution.py:17
  139.2 6.3 %collective-permute-start.3 = (f32[128,512]{1,0:T(8,128)S(1)}, f32[128,512]{1,0:T(8,128)S(1)}, u32[]{:S(2)}, u32[]{:S(2)}) collective-permute-start(f32[128,512]{1,0:T(8,128)S(1)} %multiply_subtract_fusion), channel_id=1, source_target_pairs={{2,0},{4,2},{6,4},{8,6},{10,8},{12,10},{14,12},{16,14},{18,16},{20... | collective-permute-start | bytes 786440 | tf_op jit(solution)/shard_map/ppermute | solution.py:17
Sparse Core Ops, SparseCore 0:
  12.2 24.8 all-reduce.4
  46.3 24.4 all-reduce.6
  80.0 24.4 all-reduce.8
  113.7 24.4 all-reduce.10
where the time goes:
time: 155 us; the launch traced here: 153 us
  waiting for transfers between devices  111 us (72%)
  between operations  13.9 us (9%)
  matrix products  10.4 us (7%)
  other arithmetic  9.76 us (6%)
  starting transfers between devices  4.89 us (3%)
  local copies, waits for them, and re-layouts  2.46 us (2%)
    psum x4, waiting for transfers between devices, local(): total_grad = lax.psum(partial_grad, 'split')  97.8 us
    ppermute x4, waiting for transfers between devices, passed_along(): return lax.ppermute(block, axis, route)  13.3 us
    reduce_sum x4, other arithmetic, dense_counts(): return jnp.sum(hits, axis=1)  4.99 us
    ppermute x4, starting transfers between devices, passed_along(): return lax.ppermute(block, axis, route)  4.73 us
    dot_general x4, matrix products, block_step(): lax.dot_general(errors, user_rows, (((0,), (0,)), ((), ())), precision=la...  4.64 us
    sub x4, other arithmetic, local(): held = held - LEARN_RATE * (total_grad + RIDGE_COEF * held)  4.01 us
    dot_general x4, matrix products, block_step(): jnp.dot(errors, held, precision=lax.Precision.HIGHEST, preferred_element_...  3.43 us
  transfers between devices with their start and end apart: 8, of which 8 were waited for; matrix products, arithmetic and copies ran while one was open for 5% of the time, Pallas kernels for 0%

commit v1 on v0

v1 whole, which is shorter than its diff:
```python
import functools

import jax
import jax.numpy as jnp
from jax import lax
from jax.experimental import pallas as pl
from jax.experimental.pallas import tpu as pltpu
from jax.sharding import PartitionSpec as P

SUBS = 4


LEARN_RATE = 0.0005
CONF_SCALE = 0.5
RIDGE_COEF = 0.01

MESH = pl.DeviceIdType.MESH
PIECES = 2
COLS = 2


def halves(x):
    high = x.astype(jnp.bfloat16)
    return high, (x - high.astype(jnp.float32)).astype(jnp.bfloat16)


def product(a, b, dims):
    dot = functools.partial(
        lax.dot_general, dimension_numbers=(dims, ((), ())), preferred_element_type=jnp.float32
    )
    return dot(a[0], b[0]) + (dot(a[0], b[1]) + dot(a[1], b[0]))


BOTH_LAST = ((1,), (1,))
PLAIN = ((1,), (0,))
BOTH_FIRST = ((0,), (0,))


def kernel(
    n_blk, n_split,
    u_ref, h_ref, item_ref, conf_ref, u_out, i_out,
    users, users_hi, users_lo, slab_hi, slab_lo, err_hi, err_lo, counts, grad, item_in, conf_in,
    held, outgoing, share_in, share_buf,
    obs_send, obs_recv, u_send, u_recv, h_send, h_recv, share_send, share_recv,
):
    u_dev, rank = u_ref.shape
    slab_rows = h_ref.shape[0]
    share_rows = slab_rows // n_split
    piece = u_dev // PIECES
    col = rank // COLS
    blk = lax.axis_index("blk")
    spl = lax.axis_index("split")
    ahead = lax.rem(blk + n_blk - 1, n_blk)
    behind = lax.rem(blk + 1, n_blk)
    peers = [lax.rem(spl + q, n_split) for q in range(n_split)]
    share_at = pl.multiple_of(spl * share_rows, share_rows)

    barrier = pltpu.get_barrier_semaphore()
    for other in (ahead, behind):
        pl.semaphore_signal(barrier, inc=1, device_id=(other, spl), device_id_type=MESH)
    for q in range(1, n_split):
        pl.semaphore_signal(barrier, inc=1, device_id=(blk, peers[q]), device_id_type=MESH)
    pl.semaphore_wait(barrier, n_split + 1)

    obs_copies, user_copies = [None], [None]
    for q in range(1, n_split):
        slot = n_split - q
        copies = []
        for i, (here, there) in enumerate(((item_ref, item_in), (conf_ref, conf_in))):
            copy = pltpu.make_async_remote_copy(
                src_ref=here, dst_ref=there.at[slot - 1],
                send_sem=obs_send.at[q - 1, i], recv_sem=obs_recv.at[slot - 1, i],
                device_id=(blk, peers[q]), device_id_type=MESH,
            )
            copy.start()
            copies.append(copy)
        obs_copies.append(copies)
    for q in range(1, n_split):
        slot = n_split - q
        copies = []
        for p in range(PIECES):
            copy = pltpu.make_async_remote_copy(
                src_ref=u_ref.at[pl.ds(p * piece, piece)],
                dst_ref=users.at[pl.ds(slot * u_dev + p * piece, piece)],
                send_sem=u_send.at[q - 1, p], recv_sem=u_recv.at[slot - 1, p],
                device_id=(blk, peers[q]), device_id_type=MESH,
            )
            copy.start()
            copies.append(copy)
        user_copies.append(copies)

    def count(items, confs, q):
        rows = lax.broadcasted_iota(jnp.int32, (slab_rows, u_dev), 0)
        for step in range(SUBS):
            total = jnp.zeros((slab_rows, u_dev), jnp.float32)
            for k in range(items.shape[1]):
                conf = confs[step, k:k + 1, :].astype(jnp.float32)
                total = total + jnp.where(rows == items[step, k:k + 1, :], conf, 0.0)
            counts[step, :, q * u_dev:(q + 1) * u_dev] = total

    def errors(scores, r):
        target = jnp.where(r > 0, 1.0, 0.0).astype(jnp.float32)
        return (1.0 + CONF_SCALE * r) * (scores - target)

    def split_users(rows):
        high, low = halves(users[rows, :])
        users_hi[rows, :] = high
        users_lo[rows, :] = low

    def split_slab(slab, columns):
        high, low = halves(slab[:, columns])
        slab_hi[:, columns] = high
        slab_lo[:, columns] = low

    def scores_of(rows):
        return product(
            (slab_hi[...], slab_lo[...]), (users_hi[rows, :], users_lo[rows, :]), BOTH_LAST
        )

    def keep_errors(step, rows, scores):
        high, low = halves(errors(scores, counts[step, :, rows]))
        err_hi[:, rows] = high
        err_lo[:, rows] = low

    def item_grad(rows, columns):
        return product(
            (err_hi[:, rows], err_lo[:, rows]),
            (users_hi[rows, columns], users_lo[rows, columns]),
            PLAIN,
        )

    def user_step(rows):
        grad_user = product(
            (err_hi[:, rows], err_lo[:, rows]), (slab_hi[...], slab_lo[...]), BOTH_FIRST
        )
        old = users[rows, :]
        return old - LEARN_RATE * (grad_user + RIDGE_COEF * old)

    def send_slab(step, slab, c, total):
        columns = slice(c * col, (c + 1) * col)
        old = slab[:, columns]
        outgoing[step, c] = old - LEARN_RATE * (total + RIDGE_COEF * old)
        copy = pltpu.make_async_remote_copy(
            src_ref=outgoing.at[step, c], dst_ref=held.at[step, :, pl.ds(c * col, col)],
            send_sem=h_send.at[step, c], recv_sem=h_recv.at[step, c],
            device_id=(ahead, spl), device_id_type=MESH,
        )
        copy.start()
        return copy

    every = slice(0, n_split * u_dev)
    own = slice(0, u_dev)
    slab_copies = []

    users[own, :] = u_ref[...]
    split_users(own)
    split_slab(h_ref, slice(0, rank))
    count(item_ref, conf_ref, 0)
    keep_errors(0, own, scores_of(own))
    grad[...] = item_grad(own, slice(0, rank))
    for q in range(1, n_split):
        for copy in obs_copies[n_split - q]:
            copy.wait_recv()
        count(item_in.at[q - 1], conf_in.at[q - 1], q)
    for q in range(1, n_split):
        for p in range(PIECES):
            user_copies[n_split - q][p].wait_recv()
            rows = slice(q * u_dev + p * piece, q * u_dev + (p + 1) * piece)
            split_users(rows)
            keep_errors(0, rows, scores_of(rows))
            if q < n_split - 1 or p < PIECES - 1:
                grad[...] += item_grad(rows, slice(0, rank))
    for c in range(COLS):
        columns = slice(c * col, (c + 1) * col)
        total = grad[:, columns] + item_grad(rows, columns)
        slab_copies.append(send_slab(0, h_ref, c, total))

    def update_users():
        for q in range(n_split):
            rows = slice(q * u_dev, (q + 1) * u_dev)
            users[rows, :] = user_step(rows)
            split_users(rows)

    update_users()

    for step in range(1, SUBS):
        slab = held.at[step - 1]
        last = step == SUBS - 1
        for c in range(COLS):
            slab_copies[(step - 1) * COLS + c].wait_recv()
            split_slab(slab, slice(c * col, (c + 1) * col))
        if not last:
            keep_errors(step, every, scores_of(every))
            for c in range(COLS):
                columns = slice(c * col, (c + 1) * col)
                slab_copies.append(send_slab(step, slab, c, item_grad(every, columns)))
            update_users()
        else:
            keep_errors(step, own, scores_of(own))
            share = pl.ds(share_at, share_rows)
            total = product(
                (err_hi[share, own], err_lo[share, own]),
                (users_hi[own, :], users_lo[own, :]),
                PLAIN,
            )
            others = slice(u_dev, n_split * u_dev)
            scores = product(
                (slab_hi[share, :], slab_lo[share, :]),
                (users_hi[others, :], users_lo[others, :]),
                BOTH_LAST,
            )
            total = total + product(
                halves(errors(scores, counts[step, share, others])),
                (users_hi[others, :], users_lo[others, :]),
                PLAIN,
            )
            old = slab[share, :]
            share_buf[...] = old - LEARN_RATE * (total + RIDGE_COEF * old)
            share_copy = pltpu.make_async_remote_copy(
                src_ref=share_buf, dst_ref=share_in, send_sem=share_send, recv_sem=share_recv,
                device_id=(ahead, spl), device_id_type=MESH,
            )
            share_copy.start()
            u_out[...] = user_step(own)
    for q in range(1, n_split):
        for copy in obs_copies[q]:
            copy.wait_send()
        for p in range(PIECES):
            user_copies[q][p].wait_send()
    for slab_copy in slab_copies:
        slab_copy.wait_send()
    share_copy.wait_send()
    share_copy.wait_recv()
    i_out[...] = share_in[...]


def local(n_blk, n_split, user_factors, item_factors, obs_items, obs_conf):
    u_dev, rank = user_factors.shape
    slab_rows = item_factors.shape[0]
    share_rows = slab_rows // n_split
    subs = obs_items.shape[1]
    items, confs = (obs.transpose(1, 2, 0) for obs in (obs_items, obs_conf))
    everyone = n_split * u_dev
    f32, b16 = jnp.float32, jnp.bfloat16
    dma = pltpu.SemaphoreType.DMA
    return pl.pallas_call(
        functools.partial(kernel, n_blk, n_split),
        out_shape=(
            jax.ShapeDtypeStruct((u_dev, rank), f32),
            jax.ShapeDtypeStruct((share_rows, rank), f32),
        ),
        in_specs=[pl.BlockSpec(memory_space=pltpu.VMEM)] * 4,
        out_specs=(pl.BlockSpec(memory_space=pltpu.VMEM),) * 2,
        scratch_shapes=[
            pltpu.VMEM((everyone, rank), f32),
            pltpu.VMEM((everyone, rank), b16),
            pltpu.VMEM((everyone, rank), b16),
            pltpu.VMEM((slab_rows, rank), b16),
            pltpu.VMEM((slab_rows, rank), b16),
            pltpu.VMEM((slab_rows, everyone), b16),
            pltpu.VMEM((slab_rows, everyone), b16),
            pltpu.VMEM((subs, slab_rows, everyone), f32),
            pltpu.VMEM((slab_rows, rank), f32),
            pltpu.VMEM((n_split - 1,) + items.shape, jnp.int32),
            pltpu.VMEM((n_split - 1,) + items.shape, jnp.int32),
            pltpu.VMEM((subs - 1, slab_rows, rank), f32),
            pltpu.VMEM((subs - 1, COLS, slab_rows, rank // COLS), f32),
            pltpu.VMEM((share_rows, rank), f32),
            pltpu.VMEM((share_rows, rank), f32),
            dma((n_split - 1, 2)),
            dma((n_split - 1, 2)),
            dma((n_split - 1, PIECES)),
            dma((n_split - 1, PIECES)),
            dma((subs - 1, COLS)),
            dma((subs - 1, COLS)),
            dma,
            dma,
        ],
        compiler_params=pltpu.CompilerParams(
            collective_id=0, has_side_effects=True, vmem_limit_bytes=48 * 2**20
        ),
    )(user_factors, item_factors, items, confs)


def solution(mesh):
    in_specs = (
        P(("blk", "split"), None),
        P("blk", None),
        P(("blk", "split"), None, None),
        P(("blk", "split"), None, None),
    )
    out_specs = (P(("blk", "split"), None), P(("blk", "split"), None))
    body = functools.partial(local, mesh.shape["blk"], mesh.shape["split"])
    return jax.shard_map(body, mesh=mesh, in_specs=in_specs, out_specs=out_specs, check_vma=False)
```

time: 155 us -> 41.7 us (0.27); the launches traced: 153 us -> 41 us
  waiting for transfers between devices: 111 us -> 0 us
  Pallas kernels: 0 us -> 35.4 us
  between operations: 13.9 us -> 0.65 us
  matrix products: 10.4 us -> 0 us
  other arithmetic: 9.76 us -> 0 us
  starting transfers between devices: 4.89 us -> 0 us
  local copies, waits for them, and re-layouts: 2.46 us -> 4.95 us
    psum x4 -> x0, waiting for transfers between devices: 97.8 us -> none  [local(): total_grad = lax.psum(partial_grad, 'split')]
    pallas_call x0 -> x1, Pallas kernels: none -> 35.4 us  [local(): pl.pallas_call(functools.partial(kernel, n_blk, n_split), out_shape=(jax....]
    ppermute x4 -> x0, waiting for transfers between devices: 13.3 us -> none  [passed_along(): return lax.ppermute(block, axis, route)]
    dot_general x12 -> x0, matrix products: 10.4 us -> none  [the longest x4 4.64 us: block_step(): lax.dot_general(errors, user_rows, (((0,), (0,)), ((), ())), precision=la...]
    reduce_sum x4 -> x0, other arithmetic: 4.99 us -> none  [dense_counts(): return jnp.sum(hits, axis=1)]
    unnamed x4 -> x10, local copies, waits for them, and re-layouts: 0.01 us -> 4.95 us
    ppermute x4 -> x0, starting transfers between devices: 4.73 us -> none  [passed_along(): return lax.ppermute(block, axis, route)]
    sub x4 -> x0, other arithmetic: 4.01 us -> none  [local(): held = held - LEARN_RATE * (total_grad + RIDGE_COEF * held)]
  transfers between devices with their start and end apart: 8 -> 0, of which waited for: 8 -> 0; matrix products, arithmetic and copies ran while one was open for 5% -> 0% of each run, Pallas kernels for 0% -> 0%
where the time goes in v1:
time: 41.7 us; the launch traced here: 41 us
  Pallas kernels  35.4 us (85%)
  local copies, waits for them, and re-layouts  4.95 us (12%)
  between operations  0.65 us (2%)
    pallas_call x1, Pallas kernels, local(): pl.pallas_call(functools.partial(kernel, n_blk, n_split), out_shape=(jax....  35.4 us
    unnamed x10, local copies, waits for them, and re-layouts  4.95 us

profile of v1, /device:TPU:1, one launch (start us, length us, event | category | flops | bytes accessed | tf_op | source)
XLA Modules:
  0.0 41.0 jit_solution(5919767332919829961)
XLA Ops:
  0.6 0.0 copy-start
  0.6 1.0 %copy-done = f32[256,512]{1,0:T(8,128)S(1)} copy-done((f32[256,512]{1,0:T(8,128)S(1)}, f32[256,512]{1,0:T(8,128)}, u32[]{:S(2)}) %copy-start) | copy-done | bytes 524312
  1.7 0.0 copy-start.1
  1.7 0.9 %copy-done.1 = f32[128,512]{1,0:T(8,128)S(1)} copy-done((f32[128,512]{1,0:T(8,128)S(1)}, f32[128,512]{1,0:T(8,128)}, u32[]{:S(2)}) %copy-start.1) | copy-done | bytes 262168
  2.6 0.0 copy-start.2
  2.6 0.8 %copy-done.2 = s32[256,4,8]{0,2,1:T(8,128)S(1)} copy-done((s32[256,4,8]{0,2,1:T(8,128)S(1)}, s32[256,4,8]{0,2,1:T(8,128)}, u32[]{:S(2)}) %copy-start.2) | copy-done | bytes 32792
  3.4 0.0 copy-start.3
  3.4 0.8 %copy-done.3 = s32[256,4,8]{0,2,1:T(8,128)S(1)} copy-done((s32[256,4,8]{0,2,1:T(8,128)S(1)}, s32[256,4,8]{0,2,1:T(8,128)}, u32[]{:S(2)}) %copy-start.3) | copy-done | bytes 32792
  4.1 35.4 %shard_map.59 = (f32[256,512]{1,0:T(8,128)S(1)}, f32[64,512]{1,0:T(8,128)S(1)}) custom-call(f32[256,512]{1,0:T(8,128)S(1)} %copy-done, f32[128,512]{1,0:T(8,128)S(1)} %copy-done.1, s32[4,8,256]{2,1,0:T(8,128)S(1)} %bitcast.2, s32[4,8,256]{2,1,0:T(8,128)S(1)} %bitcast.3), custom_call_target="tpu_custom_call" | custom-call | tf_op jit(solution)/shard_map/pallas_call | solution.py:246
  39.6 0.8 %copy.8 = f32[256,512]{1,0:T(8,128)} copy(f32[256,512]{1,0:T(8,128)S(1)} %get-tuple-element.4) | data formatting | bytes 1048576
  40.4 0.7 %copy.9 = f32[64,512]{1,0:T(8,128)} copy(f32[64,512]{1,0:T(8,128)S(1)} %get-tuple-element.5) | data formatting | bytes 262144
Async XLA Ops:
  0.6 1.0 %copy-start = (f32[256,512]{1,0:T(8,128)S(1)}, f32[256,512]{1,0:T(8,128)}, u32[]{:S(2)}) copy-start(f32[256,512]{1,0:T(8,128)} %u_ref.1) | copy-start | bytes 1572868
  1.7 0.9 %copy-start.1 = (f32[128,512]{1,0:T(8,128)S(1)}, f32[128,512]{1,0:T(8,128)}, u32[]{:S(2)}) copy-start(f32[128,512]{1,0:T(8,128)} %h_ref.1) | copy-start | bytes 786436
  2.6 0.8 %copy-start.2 = (s32[256,4,8]{0,2,1:T(8,128)S(1)}, s32[256,4,8]{0,2,1:T(8,128)}, u32[]{:S(2)}) copy-start(s32[256,4,8]{0,2,1:T(8,128)} %param.6) | copy-start | bytes 98308
  3.4 0.8 %copy-start.3 = (s32[256,4,8]{0,2,1:T(8,128)S(1)}, s32[256,4,8]{0,2,1:T(8,128)}, u32[]{:S(2)}) copy-start(s32[256,4,8]{0,2,1:T(8,128)} %param.7) | copy-start | bytes 98308

commit v2 on v1

v2 whole, which is shorter than its diff:
```python
import functools

import jax
import jax.numpy as jnp
from jax import lax
from jax.experimental import pallas as pl
from jax.experimental.pallas import tpu as pltpu
from jax.sharding import PartitionSpec as P

SUBS = 4


LEARN_RATE = 0.0005
CONF_SCALE = 0.5
RIDGE_COEF = 0.01

MESH = pl.DeviceIdType.MESH
PIECES = 2
COLS = 2


def halves(x):
    high = x.astype(jnp.bfloat16)
    return high, (x - high.astype(jnp.float32)).astype(jnp.bfloat16)


def dot(a, b, dims):
    return lax.dot_general(a, b, (dims, ((), ())), preferred_element_type=jnp.float32)


def stacked(a, b, dims):
    rows = a.shape[0] // 2
    both = dot(a, b[0], dims)
    return both[:rows] + (both[rows:] + dot(a[:rows], b[1], dims))


BOTH_LAST = ((1,), (1,))
PLAIN = ((1,), (0,))
BOTH_FIRST = ((0,), (0,))


def kernel(
    n_blk, n_split,
    u_hbm, h_hbm, item_hbm, conf_hbm, u_out, i_out,
    users, users_hi, users_lo, slab_16, err_16, counts, grad, item_in, conf_in,
    held, outgoing, share_buf,
    load_sem, obs_send, obs_recv, u_send, u_recv, h_send, h_recv, share_send, share_recv,
):
    u_dev, rank = u_hbm.shape
    slab_rows = h_hbm.shape[0]
    share_rows = slab_rows // n_split
    piece = u_dev // PIECES
    col = rank // COLS
    blk = lax.axis_index("blk")
    spl = lax.axis_index("split")
    ahead = lax.rem(blk + n_blk - 1, n_blk)
    behind = lax.rem(blk + 1, n_blk)
    peers = [lax.rem(spl + q, n_split) for q in range(n_split)]
    share_at = pl.multiple_of(spl * share_rows, share_rows)

    barrier = pltpu.get_barrier_semaphore()
    for q in range(1, n_split):
        pl.semaphore_signal(barrier, inc=1, device_id=(blk, peers[q]), device_id_type=MESH)
    for other in (ahead, behind):
        pl.semaphore_signal(barrier, inc=1, device_id=(other, spl), device_id_type=MESH)
    loads = [
        pltpu.make_async_copy(there, here, load_sem.at[i])
        for i, (there, here) in enumerate((
            (u_hbm, users.at[pl.ds(0, u_dev)]),
            (h_hbm, held.at[0]),
            (item_hbm, item_in.at[0]),
            (conf_hbm, conf_in.at[0]),
        ))
    ]
    for load in loads:
        load.start()
    pl.semaphore_wait(barrier, n_split + 1)

    def send_obs(q, part, steps):
        slot = n_split - q
        copies = []
        for i, (here, there) in enumerate(((item_hbm, item_in), (conf_hbm, conf_in))):
            copy = pltpu.make_async_remote_copy(
                src_ref=here.at[steps], dst_ref=there.at[slot, steps],
                send_sem=obs_send.at[q - 1, part, i], recv_sem=obs_recv.at[slot - 1, part, i],
                device_id=(blk, peers[q]), device_id_type=MESH,
            )
            copy.start()
            copies.append(copy)
        return copies

    first, rest = pl.ds(0, 1), pl.ds(1, SUBS - 1)
    first_obs = [None] + [send_obs(q, 0, first) for q in range(1, n_split)]
    user_copies = [None]
    for q in range(1, n_split):
        slot = n_split - q
        copies = []
        for p in range(PIECES):
            copy = pltpu.make_async_remote_copy(
                src_ref=u_hbm.at[pl.ds(p * piece, piece)],
                dst_ref=users.at[pl.ds(slot * u_dev + p * piece, piece)],
                send_sem=u_send.at[q - 1, p], recv_sem=u_recv.at[slot - 1, p],
                device_id=(blk, peers[q]), device_id_type=MESH,
            )
            copy.start()
            copies.append(copy)
        user_copies.append(copies)

    def count(q, steps):
        rows = lax.broadcasted_iota(jnp.int32, (slab_rows, u_dev), 0)
        for step in steps:
            total = jnp.zeros((slab_rows, u_dev), jnp.float32)
            for k in range(item_in.shape[2]):
                item = item_in[q, step, k:k + 1, :]
                conf = conf_in[q, step, k:k + 1, :].astype(jnp.float32)
                total = total + jnp.where(rows == item, conf, 0.0)
            counts[step, :, q * u_dev:(q + 1) * u_dev] = total

    def errors(scores, r):
        target = jnp.where(r > 0, 1.0, 0.0).astype(jnp.float32)
        return (1.0 + CONF_SCALE * r) * (scores - target)

    def split_users(rows):
        high, low = halves(users[rows, :])
        users_hi[rows, :] = high
        users_lo[rows, :] = low

    def split_slab(slab, columns):
        high, low = halves(slab[:, columns])
        slab_16[0:slab_rows, columns] = high
        slab_16[slab_rows:2 * slab_rows, columns] = low
        slab_16[2 * slab_rows:, columns] = high

    def scores_of(rows, columns):
        return stacked(
            slab_16[0:2 * slab_rows, columns],
            (users_hi[rows, columns], users_lo[rows, columns]),
            BOTH_LAST,
        )

    def keep_errors(step, rows, scores):
        high, low = halves(errors(scores, counts[step, :, rows]))
        err_16[0:slab_rows, rows] = high
        err_16[slab_rows:2 * slab_rows, rows] = high
        err_16[2 * slab_rows:, rows] = low

    def item_grad(rows, columns):
        return stacked(
            err_16[slab_rows:, rows], (users_hi[rows, columns], users_lo[rows, columns]), PLAIN
        )

    def user_step(rows):
        grad_user = dot(err_16[:, rows], slab_16[...], BOTH_FIRST)
        old = users[rows, :]
        return old - LEARN_RATE * (grad_user + RIDGE_COEF * old)

    def send_slab(step, c, total):
        columns = slice(c * col, (c + 1) * col)
        old = held[step, :, columns]
        outgoing[step, c] = old - LEARN_RATE * (total + RIDGE_COEF * old)
        copy = pltpu.make_async_remote_copy(
            src_ref=outgoing.at[step, c], dst_ref=held.at[step + 1, :, pl.ds(c * col, col)],
            send_sem=h_send.at[step, c], recv_sem=h_recv.at[step, c],
            device_id=(ahead, spl), device_id_type=MESH,
        )
        copy.start()
        return copy

    whole = slice(0, rank)
    every = slice(0, n_split * u_dev)
    own = slice(0, u_dev)
    columns_of = [slice(c * col, (c + 1) * col) for c in range(COLS)]
    slab_copies = []

    for load in loads:
        load.wait()
    split_users(own)
    split_slab(held.at[0], whole)
    count(0, range(SUBS))
    keep_errors(0, own, scores_of(own, whole))
    grad[...] = item_grad(own, whole)
    for q in range(1, n_split):
        for copy in first_obs[n_split - q]:
            copy.wait_recv()
        count(q, range(1))
    rest_obs = [None]
    for q in range(1, n_split):
        for p in range(PIECES):
            user_copies[n_split - q][p].wait_recv()
            rows = slice(q * u_dev + p * piece, q * u_dev + (p + 1) * piece)
            split_users(rows)
            keep_errors(0, rows, scores_of(rows, whole))
            if q < n_split - 1 or p < PIECES - 1:
                grad[...] += item_grad(rows, whole)
    for c, columns in enumerate(columns_of):
        slab_copies.append(send_slab(0, c, grad[:, columns] + item_grad(rows, columns)))
    for q in range(1, n_split):
        rest_obs.append(send_obs(q, 1, rest))

    def update_users():
        for q in range(n_split):
            rows = slice(q * u_dev, (q + 1) * u_dev)
            users[rows, :] = user_step(rows)
            split_users(rows)

    update_users()
    for q in range(1, n_split):
        for copy in rest_obs[n_split - q]:
            copy.wait_recv()
        count(q, range(1, SUBS))

    for step in range(1, SUBS - 1):
        scores = 0.0
        for c, columns in enumerate(columns_of):
            slab_copies[(step - 1) * COLS + c].wait_recv()
            split_slab(held.at[step], columns)
            scores = scores + scores_of(every, columns)
        keep_errors(step, every, scores)
        for c, columns in enumerate(columns_of):
            slab_copies.append(send_slab(step, c, item_grad(every, columns)))
        update_users()

    last = SUBS - 1
    share = pl.ds(share_at, share_rows)
    low_share = pl.ds(pl.multiple_of(slab_rows + share_at, share_rows), share_rows)
    scores = 0.0
    for c, columns in enumerate(columns_of):
        slab_copies[(last - 1) * COLS + c].wait_recv()
        split_slab(held.at[last], columns)
        scores = scores + stacked(
            jnp.concatenate([slab_16[share, columns], slab_16[low_share, columns]], axis=0),
            (users_hi[:, columns], users_lo[:, columns]),
            BOTH_LAST,
        )
    share_errors = jnp.concatenate(halves(errors(scores, counts[last, share, :])), axis=0)
    total = stacked(share_errors, (users_hi[...], users_lo[...]), PLAIN)
    old = held[last, share, :]
    share_buf[...] = old - LEARN_RATE * (total + RIDGE_COEF * old)
    share_copy = pltpu.make_async_remote_copy(
        src_ref=share_buf, dst_ref=i_out, send_sem=share_send, recv_sem=share_recv,
        device_id=(ahead, spl), device_id_type=MESH,
    )
    share_copy.start()
    keep_errors(last, own, scores_of(own, whole))
    users[own, :] = user_step(own)
    store = pltpu.make_async_copy(users.at[pl.ds(0, u_dev)], u_out, load_sem.at[0])
    store.start()

    for q in range(1, n_split):
        for copy in first_obs[q] + rest_obs[q] + user_copies[q]:
            copy.wait_send()
    for copy in slab_copies:
        copy.wait_send()
    share_copy.wait_send()
    share_copy.wait_recv()
    store.wait()


def local(n_blk, n_split, user_factors, item_factors, obs_items, obs_conf):
    u_dev, rank = user_factors.shape
    slab_rows = item_factors.shape[0]
    share_rows = slab_rows // n_split
    subs = obs_items.shape[1]
    items, confs = (obs.transpose(1, 2, 0) for obs in (obs_items, obs_conf))
    everyone = n_split * u_dev
    f32, b16 = jnp.float32, jnp.bfloat16
    dma = pltpu.SemaphoreType.DMA
    return pl.pallas_call(
        functools.partial(kernel, n_blk, n_split),
        out_shape=(
            jax.ShapeDtypeStruct((u_dev, rank), f32),
            jax.ShapeDtypeStruct((share_rows, rank), f32),
        ),
        in_specs=[pl.BlockSpec(memory_space=pltpu.HBM)] * 4,
        out_specs=(pl.BlockSpec(memory_space=pl.ANY),) * 2,
        scratch_shapes=[
            pltpu.VMEM((everyone, rank), f32),
            pltpu.VMEM((everyone, rank), b16),
            pltpu.VMEM((everyone, rank), b16),
            pltpu.VMEM((3 * slab_rows, rank), b16),
            pltpu.VMEM((3 * slab_rows, everyone), b16),
            pltpu.VMEM((subs, slab_rows, everyone), f32),
            pltpu.VMEM((slab_rows, rank), f32),
            pltpu.VMEM((n_split,) + items.shape, jnp.int32),
            pltpu.VMEM((n_split,) + items.shape, jnp.int32),
            pltpu.VMEM((subs, slab_rows, rank), f32),
            pltpu.VMEM((subs - 1, COLS, slab_rows, rank // COLS), f32),
            pltpu.VMEM((share_rows, rank), f32),
            dma((4,)),
            dma((n_split - 1, 2, 2)),
            dma((n_split - 1, 2, 2)),
            dma((n_split - 1, PIECES)),
            dma((n_split - 1, PIECES)),
            dma((subs - 1, COLS)),
            dma((subs - 1, COLS)),
            dma,
            dma,
        ],
        compiler_params=pltpu.CompilerParams(
            collective_id=0, has_side_effects=True, vmem_limit_bytes=63 * 2**20
        ),
    )(user_factors, item_factors, items, confs)


def solution(mesh):
    in_specs = (
        P(("blk", "split"), None),
        P("blk", None),
        P(("blk", "split"), None, None),
        P(("blk", "split"), None, None),
    )
    out_specs = (P(("blk", "split"), None), P(("blk", "split"), None))
    body = functools.partial(local, mesh.shape["blk"], mesh.shape["split"])
    return jax.shard_map(body, mesh=mesh, in_specs=in_specs, out_specs=out_specs, check_vma=False)
```

time: 41.7 us -> 37.8 us (0.906); the launches traced: 41 us -> 37.6 us
  local copies, waits for them, and re-layouts: 4.95 us -> 2.56 us
  Pallas kernels: 35.4 us -> 34.4 us
    unnamed x10 -> x4, local copies, waits for them, and re-layouts: 4.95 us -> 2.56 us
    pallas_call x1, Pallas kernels: 35.4 us -> 34.4 us  [local(): pl.pallas_call(functools.partial(kernel, n_blk, n_split), out_shape=(jax....]
where the time goes in v2:
time: 37.8 us; the launch traced here: 37.6 us
  Pallas kernels  34.4 us (91%)
  local copies, waits for them, and re-layouts  2.56 us (7%)
  between operations  0.65 us (2%)
    pallas_call x1, Pallas kernels, local(): pl.pallas_call(functools.partial(kernel, n_blk, n_split), out_shape=(jax....  34.4 us
    unnamed x4, local copies, waits for them, and re-layouts  2.56 us

profile of v2, /device:TPU:1, one launch (start us, length us, event | category | flops | bytes accessed | tf_op | source)
XLA Modules:
  0.0 37.6 jit_solution(10011364485532508611)
XLA Ops:
  0.6 34.4 %shard_map.59 = (f32[256,512]{1,0:T(8,128)}, f32[64,512]{1,0:T(8,128)}) custom-call(f32[256,512]{1,0:T(8,128)} %u_hbm.1, f32[128,512]{1,0:T(8,128)} %h_hbm.1, s32[4,8,256]{2,1,0:T(8,128)} %bitcast.2, s32[4,8,256]{2,1,0:T(8,128)} %bitcast.3), custom_call_target="tpu_custom_call" | custom-call | tf_op jit(solution)/shard_map/pallas_call | solution.py:268
  35.1 0.0 copy-start
  35.1 1.9 %copy.8 = f32[256,512]{1,0:T(8,128)} copy(f32[256,512]{1,0:T(8,128)} %get-tuple-element.4) | data formatting | bytes 1048576
  37.0 0.0 copy-done
  37.0 0.7 %copy.9 = f32[64,512]{1,0:T(8,128)} copy(f32[64,512]{1,0:T(8,128)S(1)} %copy-done) | data formatting | bytes 262144
Async XLA Ops:
  35.1 1.9 %copy-start = (f32[64,512]{1,0:T(8,128)S(1)}, f32[64,512]{1,0:T(8,128)}, u32[]{:S(2)}) copy-start(f32[64,512]{1,0:T(8,128)} %get-tuple-element.5) | copy-start | bytes 393220

commit v3 on v2

--- a/solution.py
+++ b/solution.py
@@ -15,7 +15,8 @@
 RIDGE_COEF = 0.01
 
 MESH = pl.DeviceIdType.MESH
-PIECES = 2
+PIECES = 4
+PARTS = 2
 COLS = 2
 
 
@@ -44,7 +45,7 @@
     u_hbm, h_hbm, item_hbm, conf_hbm, u_out, i_out,
     users, users_hi, users_lo, slab_16, err_16, counts, grad, item_in, conf_in,
     held, outgoing, share_buf,
-    load_sem, obs_send, obs_recv, u_send, u_recv, h_send, h_recv, share_send, share_recv,
+    load_sem, turn_sem, obs_send, obs_recv, u_send, u_recv, h_send, h_recv, share_send, share_recv,
 ):
     u_dev, rank = u_hbm.shape
     slab_rows = h_hbm.shape[0]
@@ -91,20 +92,27 @@
 
     first, rest = pl.ds(0, 1), pl.ds(1, SUBS - 1)
     first_obs = [None] + [send_obs(q, 0, first) for q in range(1, n_split)]
-    user_copies = [None]
-    for q in range(1, n_split):
-        slot = n_split - q
-        copies = []
-        for p in range(PIECES):
-            copy = pltpu.make_async_remote_copy(
+    user_copies = [None] + [
+        [
+            pltpu.make_async_remote_copy(
                 src_ref=u_hbm.at[pl.ds(p * piece, piece)],
-                dst_ref=users.at[pl.ds(slot * u_dev + p * piece, piece)],
-                send_sem=u_send.at[q - 1, p], recv_sem=u_recv.at[slot - 1, p],
+                dst_ref=users.at[pl.ds((n_split - q) * u_dev + p * piece, piece)],
+                send_sem=u_send.at[q - 1, p], recv_sem=u_recv.at[n_split - q - 1, p],
                 device_id=(blk, peers[q]), device_id_type=MESH,
             )
-            copy.start()
-            copies.append(copy)
-        user_copies.append(copies)
+            for p in range(PIECES)
+        ]
+        for q in range(1, n_split)
+    ]
+
+    def send_users():
+        for q in range(1, n_split):
+            for copy in user_copies[q]:
+                copy.start()
+
+    paired = n_blk % 2 == 0
+    even = lax.rem(blk, 2) == 0 if paired else blk >= 0
+    pl.when(even)(send_users)
 
     def count(q, steps):
         rows = lax.broadcasted_iota(jnp.int32, (slab_rows, u_dev), 0)
@@ -183,15 +191,33 @@
         for copy in first_obs[n_split - q]:
             copy.wait_recv()
         count(q, range(1))
+    if paired:
+
+        @pl.when(jnp.logical_not(even))
+        def _():
+            pl.semaphore_wait(turn_sem, 1)
+            send_users()
+
     rest_obs = [None]
+    part = u_dev // PARTS
     for q in range(1, n_split):
         for p in range(PIECES):
             user_copies[n_split - q][p].wait_recv()
-            rows = slice(q * u_dev + p * piece, q * u_dev + (p + 1) * piece)
-            split_users(rows)
-            keep_errors(0, rows, scores_of(rows, whole))
-            if q < n_split - 1 or p < PIECES - 1:
-                grad[...] += item_grad(rows, whole)
+            if paired and q == n_split - 1 and p == PIECES - 2:
+
+                @pl.when(even)
+                def _():
+                    pl.semaphore_signal(
+                        turn_sem, inc=1, device_id=(behind, spl), device_id_type=MESH
+                    )
+
+            done = (p + 1) * piece
+            if done % part == 0:
+                rows = slice(q * u_dev + done - part, q * u_dev + done)
+                split_users(rows)
+                keep_errors(0, rows, scores_of(rows, whole))
+                if q < n_split - 1 or p < PIECES - 1:
+                    grad[...] += item_grad(rows, whole)
     for c, columns in enumerate(columns_of):
         slab_copies.append(send_slab(0, c, grad[:, columns] + item_grad(rows, columns)))
     for q in range(1, n_split):
@@ -256,6 +282,17 @@
     store.wait()
 
 
+def store_kernel(u_in, i_in, u_out, i_out, sems):
+    copies = [
+        pltpu.make_async_copy(u_in, u_out, sems.at[0]),
+        pltpu.make_async_copy(i_in, i_out, sems.at[1]),
+    ]
+    for copy in copies:
+        copy.start()
+    for copy in copies:
+        copy.wait()
+
+
 def local(n_blk, n_split, user_factors, item_factors, obs_items, obs_conf):
     u_dev, rank = user_factors.shape
     slab_rows = item_factors.shape[0]
@@ -265,7 +302,7 @@
     everyone = n_split * u_dev
     f32, b16 = jnp.float32, jnp.bfloat16
     dma = pltpu.SemaphoreType.DMA
-    return pl.pallas_call(
+    results = pl.pallas_call(
         functools.partial(kernel, n_blk, n_split),
         out_shape=(
             jax.ShapeDtypeStruct((u_dev, rank), f32),
@@ -287,6 +324,7 @@
             pltpu.VMEM((subs - 1, COLS, slab_rows, rank // COLS), f32),
             pltpu.VMEM((share_rows, rank), f32),
             dma((4,)),
+            pltpu.SemaphoreType.REGULAR,
             dma((n_split - 1, 2, 2)),
             dma((n_split - 1, 2, 2)),
             dma((n_split - 1, PIECES)),
@@ -300,6 +338,14 @@
             collective_id=0, has_side_effects=True, vmem_limit_bytes=63 * 2**20
         ),
     )(user_factors, item_factors, items, confs)
+    return pl.pallas_call(
+        store_kernel,
+        out_shape=tuple(jax.ShapeDtypeStruct(x.shape, x.dtype) for x in results),
+        in_specs=[pl.BlockSpec(memory_space=pl.ANY)] * 2,
+        out_specs=(pl.BlockSpec(memory_space=pl.ANY),) * 2,
+        scratch_shapes=[dma((2,))],
+        compiler_params=pltpu.CompilerParams(vmem_limit_bytes=63 * 2**20),
+    )(*results)
 
 
 def solution(mesh):

time: 37.8 us -> 55.3 us (1.46)
  Pallas kernels: 34.4 us -> 54.2 us
  local copies, waits for them, and re-layouts: 2.56 us -> 0 us
    pallas_call x0 -> x1, Pallas kernels: none -> 21 us  [local(): pl.pallas_call(store_kernel, out_shape=tuple((jax.ShapeDtypeStruct(x.shap...]
    unnamed x4 -> x0, local copies, waits for them, and re-layouts: 2.56 us -> none
    pallas_call x1, Pallas kernels: 34.4 us -> 33.2 us  [local(): pl.pallas_call(functools.partial(kernel, n_blk, n_split), out_shape=(jax....]
where the time goes in v3:
time: 55.3 us; the launch traced here: 54.8 us
  Pallas kernels  54.2 us (98%)
  between operations  0.64 us (1%)
    pallas_call x1, Pallas kernels, local(): pl.pallas_call(functools.partial(kernel, n_blk, n_split), out_shape=(jax....  33.2 us
    pallas_call x1, Pallas kernels, local(): pl.pallas_call(store_kernel, out_shape=tuple((jax.ShapeDtypeStruct(x.shap...  21 us

profile of v3, /device:TPU:1, one launch (start us, length us, event | category | flops | bytes accessed | tf_op | source)
XLA Modules:
  0.0 54.8 jit_solution(15119819455557568223)
XLA Ops:
  0.6 33.2 %shard_map.59 = (f32[256,512]{1,0:T(8,128)}, f32[64,512]{1,0:T(8,128)}) custom-call(f32[256,512]{1,0:T(8,128)} %u_hbm.1, f32[128,512]{1,0:T(8,128)} %h_hbm.1, s32[4,8,256]{2,1,0:T(8,128)} %bitcast.2, s32[4,8,256]{2,1,0:T(8,128)} %bitcast.3), custom_call_target="tpu_custom_call" | custom-call | tf_op jit(solution)/shard_map/pallas_call | solution.py:305
  33.8 21.0 %shard_map.60 = (f32[256,512]{1,0:T(8,128)}, f32[64,512]{1,0:T(8,128)}) custom-call(f32[256,512]{1,0:T(8,128)} %get-tuple-element.4.u_in, f32[64,512]{1,0:T(8,128)} %get-tuple-element.5.i_in), custom_call_target="tpu_custom_call" | custom-call | tf_op jit(solution)/shard_map/pallas_call | solution.py:341

commit v4 on v3

--- a/solution.py
+++ b/solution.py
@@ -68,9 +68,9 @@
         pltpu.make_async_copy(there, here, load_sem.at[i])
         for i, (there, here) in enumerate((
             (u_hbm, users.at[pl.ds(0, u_dev)]),
-            (h_hbm, held.at[0]),
             (item_hbm, item_in.at[0]),
             (conf_hbm, conf_in.at[0]),
+            *((h_hbm.at[:, pl.ds(c * col, col)], held.at[0, c]) for c in range(COLS)),
         ))
     ]
     for load in loads:
@@ -133,8 +133,9 @@
         users_hi[rows, :] = high
         users_lo[rows, :] = low
 
-    def split_slab(slab, columns):
-        high, low = halves(slab[:, columns])
+    def split_slab(step, c):
+        columns = columns_of[c]
+        high, low = halves(held[step, c])
         slab_16[0:slab_rows, columns] = high
         slab_16[slab_rows:2 * slab_rows, columns] = low
         slab_16[2 * slab_rows:, columns] = high
@@ -163,11 +164,10 @@
         return old - LEARN_RATE * (grad_user + RIDGE_COEF * old)
 
     def send_slab(step, c, total):
-        columns = slice(c * col, (c + 1) * col)
-        old = held[step, :, columns]
+        old = held[step, c]
         outgoing[step, c] = old - LEARN_RATE * (total + RIDGE_COEF * old)
         copy = pltpu.make_async_remote_copy(
-            src_ref=outgoing.at[step, c], dst_ref=held.at[step + 1, :, pl.ds(c * col, col)],
+            src_ref=outgoing.at[step, c], dst_ref=held.at[step + 1, c],
             send_sem=h_send.at[step, c], recv_sem=h_recv.at[step, c],
             device_id=(ahead, spl), device_id_type=MESH,
         )
@@ -183,7 +183,8 @@
     for load in loads:
         load.wait()
     split_users(own)
-    split_slab(held.at[0], whole)
+    for c in range(COLS):
+        split_slab(0, c)
     count(0, range(SUBS))
     keep_errors(0, own, scores_of(own, whole))
     grad[...] = item_grad(own, whole)
@@ -239,7 +240,7 @@
         scores = 0.0
         for c, columns in enumerate(columns_of):
             slab_copies[(step - 1) * COLS + c].wait_recv()
-            split_slab(held.at[step], columns)
+            split_slab(step, c)
             scores = scores + scores_of(every, columns)
         keep_errors(step, every, scores)
         for c, columns in enumerate(columns_of):
@@ -252,21 +253,25 @@
     scores = 0.0
     for c, columns in enumerate(columns_of):
         slab_copies[(last - 1) * COLS + c].wait_recv()
-        split_slab(held.at[last], columns)
+        split_slab(last, c)
         scores = scores + stacked(
             jnp.concatenate([slab_16[share, columns], slab_16[low_share, columns]], axis=0),
             (users_hi[:, columns], users_lo[:, columns]),
             BOTH_LAST,
         )
     share_errors = jnp.concatenate(halves(errors(scores, counts[last, share, :])), axis=0)
-    total = stacked(share_errors, (users_hi[...], users_lo[...]), PLAIN)
-    old = held[last, share, :]
-    share_buf[...] = old - LEARN_RATE * (total + RIDGE_COEF * old)
-    share_copy = pltpu.make_async_remote_copy(
-        src_ref=share_buf, dst_ref=i_out, send_sem=share_send, recv_sem=share_recv,
-        device_id=(ahead, spl), device_id_type=MESH,
-    )
-    share_copy.start()
+    share_copies = []
+    for c, columns in enumerate(columns_of):
+        total = stacked(share_errors, (users_hi[:, columns], users_lo[:, columns]), PLAIN)
+        old = held[last, c, share, :]
+        share_buf[c] = old - LEARN_RATE * (total + RIDGE_COEF * old)
+        copy = pltpu.make_async_remote_copy(
+            src_ref=share_buf.at[c], dst_ref=i_out.at[:, pl.ds(c * col, col)],
+            send_sem=share_send.at[c], recv_sem=share_recv.at[c],
+            device_id=(ahead, spl), device_id_type=MESH,
+        )
+        copy.start()
+        share_copies.append(copy)
     keep_errors(last, own, scores_of(own, whole))
     users[own, :] = user_step(own)
     store = pltpu.make_async_copy(users.at[pl.ds(0, u_dev)], u_out, load_sem.at[0])
@@ -277,20 +282,31 @@
             copy.wait_send()
     for copy in slab_copies:
         copy.wait_send()
-    share_copy.wait_send()
-    share_copy.wait_recv()
+    for copy in share_copies:
+        copy.wait_send()
+        copy.wait_recv()
     store.wait()
 
 
-def store_kernel(u_in, i_in, u_out, i_out, sems):
-    copies = [
-        pltpu.make_async_copy(u_in, u_out, sems.at[0]),
-        pltpu.make_async_copy(i_in, i_out, sems.at[1]),
+def store_kernel(u_in, i_in, u_out, i_out, u_buf, i_buf, load_sem, store_sem):
+    rows = u_in.shape[0] // PIECES
+    pieces = [(i_in, i_buf, i_out)]
+    for p in range(PIECES):
+        at = pl.ds(p * rows, rows)
+        pieces.append((u_in.at[at], u_buf.at[at], u_out.at[at]))
+    loads = [
+        pltpu.make_async_copy(there, here, load_sem.at[i]) for i, (there, here, _) in enumerate(pieces)
     ]
-    for copy in copies:
-        copy.start()
-    for copy in copies:
-        copy.wait()
+    stores = [
+        pltpu.make_async_copy(here, out, store_sem.at[i]) for i, (_, here, out) in enumerate(pieces)
+    ]
+    for load in loads:
+        load.start()
+    for load, store in zip(loads, stores):
+        load.wait()
+        store.start()
+    for store in stores:
+        store.wait()
 
 
 def local(n_blk, n_split, user_factors, item_factors, obs_items, obs_conf):
@@ -320,10 +336,10 @@
             pltpu.VMEM((slab_rows, rank), f32),
             pltpu.VMEM((n_split,) + items.shape, jnp.int32),
             pltpu.VMEM((n_split,) + items.shape, jnp.int32),
-            pltpu.VMEM((subs, slab_rows, rank), f32),
+            pltpu.VMEM((subs, COLS, slab_rows, rank // COLS), f32),
             pltpu.VMEM((subs - 1, COLS, slab_rows, rank // COLS), f32),
-            pltpu.VMEM((share_rows, rank), f32),
-            dma((4,)),
+            pltpu.VMEM((COLS, share_rows, rank // COLS), f32),
+            dma((3 + COLS,)),
             pltpu.SemaphoreType.REGULAR,
             dma((n_split - 1, 2, 2)),
             dma((n_split - 1, 2, 2)),
@@ -331,8 +347,8 @@
             dma((n_split - 1, PIECES)),
             dma((subs - 1, COLS)),
             dma((subs - 1, COLS)),
-            dma,
-            dma,
+            dma((COLS,)),
+            dma((COLS,)),
         ],
         compiler_params=pltpu.CompilerParams(
             collective_id=0, has_side_effects=True, vmem_limit_bytes=63 * 2**20
@@ -343,7 +359,11 @@
         out_shape=tuple(jax.ShapeDtypeStruct(x.shape, x.dtype) for x in results),
         in_specs=[pl.BlockSpec(memory_space=pl.ANY)] * 2,
         out_specs=(pl.BlockSpec(memory_space=pl.ANY),) * 2,
-        scratch_shapes=[dma((2,))],
+        scratch_shapes=[
+            *(pltpu.VMEM(x.shape, x.dtype) for x in results),
+            dma((PIECES + 1,)),
+            dma((PIECES + 1,)),
+        ],
         compiler_params=pltpu.CompilerParams(vmem_limit_bytes=63 * 2**20),
     )(*results)
 

time: 55.3 us -> 36.4 us (0.66)
  Pallas kernels: 54.2 us -> 35.1 us
    pallas_call x1, Pallas kernels: 21 us -> 1.91 us  [local(): pl.pallas_call(store_kernel, out_shape=tuple((jax.ShapeDtypeStruct(x.shap...]
where the time goes in v4:
time: 36.4 us; the launch traced here: 35.8 us
  Pallas kernels  35.1 us (96%)
  between operations  0.64 us (2%)
    pallas_call x1, Pallas kernels, local(): pl.pallas_call(functools.partial(kernel, n_blk, n_split), out_shape=(jax....  33.2 us
    pallas_call x1, Pallas kernels, local(): pl.pallas_call(store_kernel, out_shape=tuple((jax.ShapeDtypeStruct(x.shap...  1.91 us

profile of v4, /device:TPU:1, one launch (start us, length us, event | category | flops | bytes accessed | tf_op | source)
XLA Modules:
  0.0 35.8 jit_solution(1886193395032441711)
XLA Ops:
  0.6 33.2 %shard_map.59 = (f32[256,512]{1,0:T(8,128)}, f32[64,512]{1,0:T(8,128)}) custom-call(f32[256,512]{1,0:T(8,128)} %u_hbm.1, f32[128,512]{1,0:T(8,128)} %h_hbm.1, s32[4,8,256]{2,1,0:T(8,128)} %bitcast.2, s32[4,8,256]{2,1,0:T(8,128)} %bitcast.3), custom_call_target="tpu_custom_call" | custom-call | tf_op jit(solution)/shard_map/pallas_call | solution.py:321
  33.8 1.9 %shard_map.60 = (f32[256,512]{1,0:T(8,128)}, f32[64,512]{1,0:T(8,128)}) custom-call(f32[256,512]{1,0:T(8,128)} %get-tuple-element.4.u_in, f32[64,512]{1,0:T(8,128)} %get-tuple-element.5.i_in), custom_call_target="tpu_custom_call" | custom-call | tf_op jit(solution)/shard_map/pallas_call | solution.py:357

commit v5 on v4

--- a/solution.py
+++ b/solution.py
@@ -77,7 +77,7 @@
         load.start()
     pl.semaphore_wait(barrier, n_split + 1)
 
-    def send_obs(q, part, steps):
+    def obs_copies(q, part, steps):
         slot = n_split - q
         copies = []
         for i, (here, there) in enumerate(((item_hbm, item_in), (conf_hbm, conf_in))):
@@ -86,12 +86,15 @@
                 send_sem=obs_send.at[q - 1, part, i], recv_sem=obs_recv.at[slot - 1, part, i],
                 device_id=(blk, peers[q]), device_id_type=MESH,
             )
-            copy.start()
             copies.append(copy)
         return copies
 
-    first, rest = pl.ds(0, 1), pl.ds(1, SUBS - 1)
-    first_obs = [None] + [send_obs(q, 0, first) for q in range(1, n_split)]
+    first, rest = pl.ds(0, 2), pl.ds(2, SUBS - 2)
+    first_obs = [None] + [obs_copies(q, 0, first) for q in range(1, n_split)]
+    rest_obs = [None] + [obs_copies(q, 1, rest) for q in range(1, n_split)]
+    for copies in first_obs[1:]:
+        for copy in copies:
+            copy.start()
     user_copies = [None] + [
         [
             pltpu.make_async_remote_copy(
@@ -114,9 +117,11 @@
     even = lax.rem(blk, 2) == 0 if paired else blk >= 0
     pl.when(even)(send_users)
 
-    def count(q, steps):
+    def count(q, start, stop):
         rows = lax.broadcasted_iota(jnp.int32, (slab_rows, u_dev), 0)
-        for step in steps:
+
+        @pl.loop(start, stop)
+        def _(step):
             total = jnp.zeros((slab_rows, u_dev), jnp.float32)
             for k in range(item_in.shape[2]):
                 item = item_in[q, step, k:k + 1, :]
@@ -163,35 +168,35 @@
         old = users[rows, :]
         return old - LEARN_RATE * (grad_user + RIDGE_COEF * old)
 
+    def slab_copy(step, c):
+        return pltpu.make_async_remote_copy(
+            src_ref=outgoing.at[step, c], dst_ref=held.at[step + 1, c],
+            send_sem=h_send.at[step, c], recv_sem=h_recv.at[step, c],
+            device_id=(ahead, spl), device_id_type=MESH,
+        )
+
     def send_slab(step, c, total):
         old = held[step, c]
         outgoing[step, c] = old - LEARN_RATE * (total + RIDGE_COEF * old)
-        copy = pltpu.make_async_remote_copy(
-            src_ref=outgoing.at[step, c], dst_ref=held.at[step + 1, c],
-            send_sem=h_send.at[step, c], recv_sem=h_recv.at[step, c],
-            device_id=(ahead, spl), device_id_type=MESH,
-        )
-        copy.start()
-        return copy
+        slab_copy(step, c).start()
 
     whole = slice(0, rank)
     every = slice(0, n_split * u_dev)
     own = slice(0, u_dev)
     columns_of = [slice(c * col, (c + 1) * col) for c in range(COLS)]
-    slab_copies = []
 
     for load in loads:
         load.wait()
     split_users(own)
     for c in range(COLS):
         split_slab(0, c)
-    count(0, range(SUBS))
+    count(0, 0, SUBS)
     keep_errors(0, own, scores_of(own, whole))
     grad[...] = item_grad(own, whole)
     for q in range(1, n_split):
         for copy in first_obs[n_split - q]:
             copy.wait_recv()
-        count(q, range(1))
+        count(q, 0, 2)
     if paired:
 
         @pl.when(jnp.logical_not(even))
@@ -199,7 +204,6 @@
             pl.semaphore_wait(turn_sem, 1)
             send_users()
 
-    rest_obs = [None]
     part = u_dev // PARTS
     for q in range(1, n_split):
         for p in range(PIECES):
@@ -220,39 +224,49 @@
                 if q < n_split - 1 or p < PIECES - 1:
                     grad[...] += item_grad(rows, whole)
     for c, columns in enumerate(columns_of):
-        slab_copies.append(send_slab(0, c, grad[:, columns] + item_grad(rows, columns)))
-    for q in range(1, n_split):
-        rest_obs.append(send_obs(q, 1, rest))
+        send_slab(0, c, grad[:, columns] + item_grad(rows, columns))
 
     def update_users():
-        for q in range(n_split):
-            rows = slice(q * u_dev, (q + 1) * u_dev)
+        @pl.loop(0, n_split)
+        def _(q):
+            rows = pl.ds(pl.multiple_of(q * u_dev, u_dev), u_dev)
             users[rows, :] = user_step(rows)
             split_users(rows)
 
     update_users()
-    for q in range(1, n_split):
-        for copy in rest_obs[n_split - q]:
-            copy.wait_recv()
-        count(q, range(1, SUBS))
-
-    for step in range(1, SUBS - 1):
+
+    @pl.loop(1, SUBS - 1)
+    def _(step):
         scores = 0.0
         for c, columns in enumerate(columns_of):
-            slab_copies[(step - 1) * COLS + c].wait_recv()
+            slab_copy(step - 1, c).wait_recv()
             split_slab(step, c)
             scores = scores + scores_of(every, columns)
         keep_errors(step, every, scores)
+
+        @pl.when(step == 1)
+        def _():
+            for copies in rest_obs[1:]:
+                for copy in copies:
+                    copy.start()
+
         for c, columns in enumerate(columns_of):
-            slab_copies.append(send_slab(step, c, item_grad(every, columns)))
+            send_slab(step, c, item_grad(every, columns))
         update_users()
+
+        @pl.when(step == 1)
+        def _():
+            for q in range(1, n_split):
+                for copy in rest_obs[n_split - q]:
+                    copy.wait_recv()
+                count(q, 2, SUBS)
 
     last = SUBS - 1
     share = pl.ds(share_at, share_rows)
     low_share = pl.ds(pl.multiple_of(slab_rows + share_at, share_rows), share_rows)
     scores = 0.0
     for c, columns in enumerate(columns_of):
-        slab_copies[(last - 1) * COLS + c].wait_recv()
+        slab_copy(last - 1, c).wait_recv()
         split_slab(last, c)
         scores = scores + stacked(
             jnp.concatenate([slab_16[share, columns], slab_16[low_share, columns]], axis=0),
@@ -280,8 +294,9 @@
     for q in range(1, n_split):
         for copy in first_obs[q] + rest_obs[q] + user_copies[q]:
             copy.wait_send()
-    for copy in slab_copies:
-        copy.wait_send()
+    for step in range(last):
+        for c in range(COLS):
+            slab_copy(step, c).wait_send()
     for copy in share_copies:
         copy.wait_send()
         copy.wait_recv()

time: 36.4 us -> 36 us (0.989)
  no operation moved by 1% of the time
where the time goes in v5:
time: 36 us; the launch traced here: 35.5 us
  Pallas kernels  34.9 us (97%)
  between operations  0.64 us (2%)
    pallas_call x1, Pallas kernels, local(): pl.pallas_call(functools.partial(kernel, n_blk, n_split), out_shape=(jax....  33 us
    pallas_call x1, Pallas kernels, local(): pl.pallas_call(store_kernel, out_shape=tuple((jax.ShapeDtypeStruct(x.shap...  1.91 us

profile of v5, /device:TPU:1, one launch (start us, length us, event | category | flops | bytes accessed | tf_op | source)
XLA Modules:
  0.0 35.5 jit_solution(13561007507403460765)
XLA Ops:
  0.6 33.0 %shard_map.59 = (f32[256,512]{1,0:T(8,128)}, f32[64,512]{1,0:T(8,128)}) custom-call(f32[256,512]{1,0:T(8,128)} %u_hbm.1, f32[128,512]{1,0:T(8,128)} %h_hbm.1, s32[4,8,256]{2,1,0:T(8,128)} %bitcast.2, s32[4,8,256]{2,1,0:T(8,128)} %bitcast.3), custom_call_target="tpu_custom_call" | custom-call | tf_op jit(solution)/shard_map/pallas_call | solution.py:336
  33.6 1.9 %shard_map.60 = (f32[256,512]{1,0:T(8,128)}, f32[64,512]{1,0:T(8,128)}) custom-call(f32[256,512]{1,0:T(8,128)} %get-tuple-element.4.u_in, f32[64,512]{1,0:T(8,128)} %get-tuple-element.5.i_in), custom_call_target="tpu_custom_call" | custom-call | tf_op jit(solution)/shard_map/pallas_call | solution.py:372

commit v6 on v5

v6 whole, which is shorter than its diff:
```python
import functools

import jax
import jax.numpy as jnp
from jax import lax
from jax.experimental import pallas as pl
from jax.experimental.pallas import tpu as pltpu
from jax.sharding import PartitionSpec as P

SUBS = 4


LEARN_RATE = 0.0005
CONF_SCALE = 0.5
RIDGE_COEF = 0.01

MESH = pl.DeviceIdType.MESH
PIECES = 4
PARTS = 2
COLS = 2


def halves(x):
    high = x.astype(jnp.bfloat16)
    return high, (x - high.astype(jnp.float32)).astype(jnp.bfloat16)


def dot(a, b, dims):
    return lax.dot_general(a, b, (dims, ((), ())), preferred_element_type=jnp.float32)


def stacked(a, b, dims):
    rows = a.shape[0] // 2
    both = dot(a, b[0], dims)
    return both[:rows] + (both[rows:] + dot(a[:rows], b[1], dims))


BOTH_LAST = ((1,), (1,))
PLAIN = ((1,), (0,))
BOTH_FIRST = ((0,), (0,))


def kernel(
    n_blk, n_split,
    u_hbm, h_hbm, item_hbm, conf_hbm, u_out, i_out,
    users, users_hi, users_lo, slab_16, err_16, counts, grad, item_in, conf_in,
    held, outgoing,
    load_sem, obs_send, obs_recv, u_send, u_recv, h_send, h_recv, share_send, share_recv,
):
    u_dev, rank = u_hbm.shape
    slab_rows = h_hbm.shape[0]
    share_rows = slab_rows // n_split
    piece = u_dev // PIECES
    col = rank // COLS
    blk = lax.axis_index("blk")
    spl = lax.axis_index("split")
    ahead = lax.rem(blk + n_blk - 1, n_blk)
    behind = lax.rem(blk + 1, n_blk)
    main = lax.rem(blk, n_split)
    is_main = spl == main
    is_side = jnp.logical_not(is_main)
    peers = [lax.rem(spl + q, n_split) for q in range(n_split)]
    takers = [lax.rem(lax.rem(ahead, n_split) + q, n_split) for q in range(n_split)]

    barrier = pltpu.get_barrier_semaphore()
    pl.semaphore_signal(
        barrier, inc=1, device_id=(behind, lax.rem(behind, n_split)), device_id_type=MESH
    )

    @pl.when(is_main)
    def _():
        for q in range(1, n_split):
            pl.semaphore_signal(barrier, inc=1, device_id=(blk, peers[q]), device_id_type=MESH)

    loads = [
        pltpu.make_async_copy(there, here, load_sem.at[i])
        for i, (there, here) in enumerate((
            (u_hbm, users.at[pl.ds(0, u_dev)]),
            (item_hbm, item_in.at[0]),
            (conf_hbm, conf_in.at[0]),
            *((h_hbm.at[:, pl.ds(c * col, col)], held.at[0, c]) for c in range(COLS)),
        ))
    ]
    for load in loads:
        load.start()
    first, rest = pl.ds(0, 2), pl.ds(2, SUBS - 2)

    def obs_copies(slot, part):
        steps = (first, rest)[part]
        return [
            pltpu.make_async_remote_copy(
                src_ref=here.at[steps], dst_ref=there.at[slot, steps],
                send_sem=obs_send.at[part, i], recv_sem=obs_recv.at[slot - 1, part, i],
                device_id=(blk, main), device_id_type=MESH,
            )
            for i, (here, there) in enumerate(((item_hbm, item_in), (conf_hbm, conf_in)))
        ]

    def user_copy(slot, p):
        at = pl.multiple_of(slot * u_dev + p * piece, piece)
        return pltpu.make_async_remote_copy(
            src_ref=u_hbm.at[pl.ds(p * piece, piece)], dst_ref=users.at[pl.ds(at, piece)],
            send_sem=u_send.at[p], recv_sem=u_recv.at[slot - 1, p],
            device_id=(blk, main), device_id_type=MESH,
        )

    my_slot = lax.rem(spl - main + n_split, n_split)

    @pl.when(is_side)
    def _():
        pl.semaphore_wait(barrier, 1)
        for copy in obs_copies(my_slot, 0):
            copy.start()
        for p in range(PIECES):
            user_copy(my_slot, p).start()

    def count(q, start, stop):
        rows = lax.broadcasted_iota(jnp.int32, (slab_rows, u_dev), 0)

        @pl.loop(start, stop)
        def _(step):
            total = jnp.zeros((slab_rows, u_dev), jnp.float32)
            for k in range(item_in.shape[2]):
                item = item_in[q, step, k:k + 1, :]
                conf = conf_in[q, step, k:k + 1, :].astype(jnp.float32)
                total = total + jnp.where(rows == item, conf, 0.0)
            counts[step, :, q * u_dev:(q + 1) * u_dev] = total

    def errors(scores, r):
        target = jnp.where(r > 0, 1.0, 0.0).astype(jnp.float32)
        return (1.0 + CONF_SCALE * r) * (scores - target)

    def split_users(rows):
        high, low = halves(users[rows, :])
        users_hi[rows, :] = high
        users_lo[rows, :] = low

    def split_slab(step, c):
        columns = columns_of[c]
        high, low = halves(held[step, c])
        slab_16[0:slab_rows, columns] = high
        slab_16[slab_rows:2 * slab_rows, columns] = low
        slab_16[2 * slab_rows:, columns] = high

    def scores_of(rows, columns):
        return stacked(
            slab_16[0:2 * slab_rows, columns],
            (users_hi[rows, columns], users_lo[rows, columns]),
            BOTH_LAST,
        )

    def keep_errors(step, rows, scores):
        high, low = halves(errors(scores, counts[step, :, rows]))
        err_16[0:slab_rows, rows] = high
        err_16[slab_rows:2 * slab_rows, rows] = high
        err_16[2 * slab_rows:, rows] = low

    def item_grad(rows, columns):
        return stacked(
            err_16[slab_rows:, rows], (users_hi[rows, columns], users_lo[rows, columns]), PLAIN
        )

    def user_step(rows):
        grad_user = dot(err_16[:, rows], slab_16[...], BOTH_FIRST)
        old = users[rows, :]
        return old - LEARN_RATE * (grad_user + RIDGE_COEF * old)

    def slab_copy(step, c, q):
        return pltpu.make_async_remote_copy(
            src_ref=outgoing.at[step, c], dst_ref=held.at[step + 1, c],
            send_sem=h_send.at[step, c, q], recv_sem=h_recv.at[step, c],
            device_id=(ahead, takers[q]), device_id_type=MESH,
        )

    def share_copy(c, q):
        at = pl.multiple_of(takers[q] * share_rows, share_rows)
        return pltpu.make_async_remote_copy(
            src_ref=outgoing.at[SUBS - 1, c, pl.ds(at, share_rows)],
            dst_ref=i_out.at[:, pl.ds(c * col, col)],
            send_sem=share_send.at[c, q], recv_sem=share_recv.at[c],
            device_id=(ahead, takers[q]), device_id_type=MESH,
        )

    def pass_on(step, copy_of, grad_of):
        for c, columns in enumerate(columns_of):
            old = held[step, c]
            outgoing[step, c] = old - LEARN_RATE * (grad_of(columns) + RIDGE_COEF * old)
            copy_of(c, 0).start()
        for q in range(1, n_split):
            for c in range(COLS):
                copy_of(c, q).start()

    whole = slice(0, rank)
    every = slice(0, n_split * u_dev)
    own = slice(0, u_dev)
    columns_of = [slice(c * col, (c + 1) * col) for c in range(COLS)]

    for load in loads:
        load.wait()
    split_users(own)
    for c in range(COLS):
        split_slab(0, c)
    count(0, 0, SUBS)
    keep_errors(0, own, scores_of(own, whole))
    last = SUBS - 1
    part = u_dev // PARTS

    def update(groups):
        @pl.loop(0, groups)
        def _(q):
            rows = pl.ds(pl.multiple_of(q * u_dev, u_dev), u_dev)
            users[rows, :] = user_step(rows)
            split_users(rows)

    def meet_slab(step, rows):
        scores = 0.0
        for c, columns in enumerate(columns_of):
            slab_copy(step - 1, c, 0).wait_recv()
            split_slab(step, c)
            scores = scores + scores_of(rows, columns)
        keep_errors(step, rows, scores)

    @pl.when(is_main)
    def _():
        grad[...] = item_grad(own, whole)
        pl.semaphore_wait(barrier, n_split)
        for q in range(1, n_split):
            for copy in obs_copies(q, 0):
                copy.wait_recv()
            count(q, 0, 2)
        for q in range(1, n_split):
            for p in range(PIECES):
                user_copy(q, p).wait_recv()
                done = (p + 1) * piece
                if done % part == 0:
                    rows = slice(q * u_dev + done - part, q * u_dev + done)
                    split_users(rows)
                    keep_errors(0, rows, scores_of(rows, whole))
                    if q < n_split - 1 or p < PIECES - 1:
                        grad[...] += item_grad(rows, whole)
        pass_on(
            0,
            functools.partial(slab_copy, 0),
            lambda columns: grad[:, columns] + item_grad(rows, columns),
        )
        update(n_split)
        for q in range(1, n_split):
            for copy in obs_copies(q, 1):
                copy.wait_recv()
            count(q, 2, SUBS)

        @pl.loop(1, last)
        def _(step):
            meet_slab(step, every)
            pass_on(step, functools.partial(slab_copy, step), functools.partial(item_grad, every))
            update(n_split)

        meet_slab(last, every)
        pass_on(last, share_copy, functools.partial(item_grad, every))

    @pl.when(is_side)
    def _():
        update(1)
        for p in range(PIECES):
            user_copy(my_slot, p).wait_send()
        for copy in obs_copies(my_slot, 1):
            copy.start()

        @pl.loop(1, last)
        def _(step):
            meet_slab(step, own)
            update(1)

        meet_slab(last, own)

    users[own, :] = user_step(own)
    store = pltpu.make_async_copy(users.at[pl.ds(0, u_dev)], u_out, load_sem.at[0])
    store.start()

    @pl.when(is_main)
    def _():
        for q in range(n_split):
            for c in range(COLS):
                for step in range(last):
                    slab_copy(step, c, q).wait_send()
                share_copy(c, q).wait_send()

    @pl.when(is_side)
    def _():
        for copy in obs_copies(my_slot, 0) + obs_copies(my_slot, 1):
            copy.wait_send()

    for c in range(COLS):
        share_copy(c, 0).wait_recv()
    store.wait()


def store_kernel(u_in, i_in, u_out, i_out, u_buf, i_buf, load_sem, store_sem):
    rows = u_in.shape[0] // PIECES
    pieces = [(i_in, i_buf, i_out)]
    for p in range(PIECES):
        at = pl.ds(p * rows, rows)
        pieces.append((u_in.at[at], u_buf.at[at], u_out.at[at]))
    loads = [
        pltpu.make_async_copy(there, here, load_sem.at[i]) for i, (there, here, _) in enumerate(pieces)
    ]
    stores = [
        pltpu.make_async_copy(here, out, store_sem.at[i]) for i, (_, here, out) in enumerate(pieces)
    ]
    for load in loads:
        load.start()
    for load, store in zip(loads, stores):
        load.wait()
        store.start()
    for store in stores:
        store.wait()


def local(n_blk, n_split, user_factors, item_factors, obs_items, obs_conf):
    u_dev, rank = user_factors.shape
    slab_rows = item_factors.shape[0]
    share_rows = slab_rows // n_split
    subs = obs_items.shape[1]
    items, confs = (obs.transpose(1, 2, 0) for obs in (obs_items, obs_conf))
    everyone = n_split * u_dev
    f32, b16 = jnp.float32, jnp.bfloat16
    dma = pltpu.SemaphoreType.DMA
    results = pl.pallas_call(
        functools.partial(kernel, n_blk, n_split),
        out_shape=(
            jax.ShapeDtypeStruct((u_dev, rank), f32),
            jax.ShapeDtypeStruct((share_rows, rank), f32),
        ),
        in_specs=[pl.BlockSpec(memory_space=pltpu.HBM)] * 4,
        out_specs=(pl.BlockSpec(memory_space=pl.ANY),) * 2,
        scratch_shapes=[
            pltpu.VMEM((everyone, rank), f32),
            pltpu.VMEM((everyone, rank), b16),
            pltpu.VMEM((everyone, rank), b16),
            pltpu.VMEM((3 * slab_rows, rank), b16),
            pltpu.VMEM((3 * slab_rows, everyone), b16),
            pltpu.VMEM((subs, slab_rows, everyone), f32),
            pltpu.VMEM((slab_rows, rank), f32),
            pltpu.VMEM((n_split,) + items.shape, jnp.int32),
            pltpu.VMEM((n_split,) + items.shape, jnp.int32),
            pltpu.VMEM((subs, COLS, slab_rows, rank // COLS), f32),
            pltpu.VMEM((subs, COLS, slab_rows, rank // COLS), f32),
            dma((3 + COLS,)),
            dma((2, 2)),
            dma((n_split - 1, 2, 2)),
            dma((PIECES,)),
            dma((n_split - 1, PIECES)),
            dma((subs - 1, COLS, n_split)),
            dma((subs - 1, COLS)),
            dma((COLS, n_split)),
            dma((COLS,)),
        ],
        compiler_params=pltpu.CompilerParams(
            collective_id=0, has_side_effects=True, vmem_limit_bytes=63 * 2**20
        ),
    )(user_factors, item_factors, items, confs)
    return pl.pallas_call(
        store_kernel,
        out_shape=tuple(jax.ShapeDtypeStruct(x.shape, x.dtype) for x in results),
        in_specs=[pl.BlockSpec(memory_space=pl.ANY)] * 2,
        out_specs=(pl.BlockSpec(memory_space=pl.ANY),) * 2,
        scratch_shapes=[
            *(pltpu.VMEM(x.shape, x.dtype) for x in results),
            dma((PIECES + 1,)),
            dma((PIECES + 1,)),
        ],
        compiler_params=pltpu.CompilerParams(vmem_limit_bytes=63 * 2**20),
    )(*results)


def solution(mesh):
    in_specs = (
        P(("blk", "split"), None),
        P("blk", None),
        P(("blk", "split"), None, None),
        P(("blk", "split"), None, None),
    )
    out_specs = (P(("blk", "split"), None), P(("blk", "split"), None))
    body = functools.partial(local, mesh.shape["blk"], mesh.shape["split"])
    return jax.shard_map(body, mesh=mesh, in_specs=in_specs, out_specs=out_specs, check_vma=False)
```

time: 36 us -> 37.1 us (1.031)
  Pallas kernels: 34.9 us -> 36.1 us
    pallas_call x1, Pallas kernels: 33 us -> 34.2 us  [local(): pl.pallas_call(functools.partial(kernel, n_blk, n_split), out_shape=(jax....]
where the time goes in v6:
time: 37.1 us; the launch traced here: 36.7 us
  Pallas kernels  36.1 us (97%)
  between operations  0.64 us (2%)
    pallas_call x1, Pallas kernels, local(): pl.pallas_call(functools.partial(kernel, n_blk, n_split), out_shape=(jax....  34.2 us
    pallas_call x1, Pallas kernels, local(): pl.pallas_call(store_kernel, out_shape=tuple((jax.ShapeDtypeStruct(x.shap...  1.91 us

profile of v6, /device:TPU:1, one launch (start us, length us, event | category | flops | bytes accessed | tf_op | source)
XLA Modules:
  0.0 36.7 jit_solution(13042043790646275490)
XLA Ops:
  0.6 34.2 %shard_map.59 = (f32[256,512]{1,0:T(8,128)}, f32[64,512]{1,0:T(8,128)}) custom-call(f32[256,512]{1,0:T(8,128)} %u_hbm.1, f32[128,512]{1,0:T(8,128)} %h_hbm.1, s32[4,8,256]{2,1,0:T(8,128)} %bitcast.2, s32[4,8,256]{2,1,0:T(8,128)} %bitcast.3), custom_call_target="tpu_custom_call" | custom-call | tf_op jit(solution)/shard_map/pallas_call | solution.py:328
  34.8 1.9 %shard_map.60 = (f32[256,512]{1,0:T(8,128)}, f32[64,512]{1,0:T(8,128)}) custom-call(f32[256,512]{1,0:T(8,128)} %get-tuple-element.4.u_in, f32[64,512]{1,0:T(8,128)} %get-tuple-element.5.i_in), custom_call_target="tpu_custom_call" | custom-call | tf_op jit(solution)/shard_map/pallas_call | solution.py:362

commit v7 on v6

--- a/solution.py
+++ b/solution.py
@@ -56,16 +56,17 @@
     spl = lax.axis_index("split")
     ahead = lax.rem(blk + n_blk - 1, n_blk)
     behind = lax.rem(blk + 1, n_blk)
-    main = lax.rem(blk, n_split)
+    def main_of(b):
+        return lax.rem((b + 1) // 2, n_split)
+
+    main = main_of(blk)
     is_main = spl == main
     is_side = jnp.logical_not(is_main)
     peers = [lax.rem(spl + q, n_split) for q in range(n_split)]
-    takers = [lax.rem(lax.rem(ahead, n_split) + q, n_split) for q in range(n_split)]
+    takers = [lax.rem(main_of(ahead) + q, n_split) for q in range(n_split)]
 
     barrier = pltpu.get_barrier_semaphore()
-    pl.semaphore_signal(
-        barrier, inc=1, device_id=(behind, lax.rem(behind, n_split)), device_id_type=MESH
-    )
+    pl.semaphore_signal(barrier, inc=1, device_id=(behind, main_of(behind)), device_id_type=MESH)
 
     @pl.when(is_main)
     def _():
@@ -186,6 +187,10 @@
             old = held[step, c]
             outgoing[step, c] = old - LEARN_RATE * (grad_of(columns) + RIDGE_COEF * old)
             copy_of(c, 0).start()
+
+    def pass_to_sides(copy_of):
+        for c in range(COLS):
+            copy_of(c, 0).wait_send()
         for q in range(1, n_split):
             for c in range(COLS):
                 copy_of(c, q).start()
@@ -244,6 +249,7 @@
             lambda columns: grad[:, columns] + item_grad(rows, columns),
         )
         update(n_split)
+        pass_to_sides(functools.partial(slab_copy, 0))
         for q in range(1, n_split):
             for copy in obs_copies(q, 1):
                 copy.wait_recv()
@@ -254,9 +260,13 @@
             meet_slab(step, every)
             pass_on(step, functools.partial(slab_copy, step), functools.partial(item_grad, every))
             update(n_split)
+            pass_to_sides(functools.partial(slab_copy, step))
 
         meet_slab(last, every)
         pass_on(last, share_copy, functools.partial(item_grad, every))
+        for q in range(1, n_split):
+            for c in range(COLS):
+                share_copy(c, q).start()
 
     @pl.when(is_side)
     def _():
@@ -279,10 +289,11 @@
 
     @pl.when(is_main)
     def _():
-        for q in range(n_split):
-            for c in range(COLS):
+        for c in range(COLS):
+            for q in range(1, n_split):
                 for step in range(last):
                     slab_copy(step, c, q).wait_send()
+            for q in range(n_split):
                 share_copy(c, q).wait_send()
 
     @pl.when(is_side)

time: 37.1 us -> 39.5 us (1.065)
  the two profiles are of different devices: /device:TPU:1 before, /device:TPU:15 now
where the time goes in v7:
time: 39.5 us; the launch traced here: 39.4 us
  Pallas kernels  38.7 us (98%)
  between operations  0.64 us (2%)
    pallas_call x1, Pallas kernels, local(): pl.pallas_call(functools.partial(kernel, n_blk, n_split), out_shape=(jax....  36.8 us
    pallas_call x1, Pallas kernels, local(): pl.pallas_call(store_kernel, out_shape=tuple((jax.ShapeDtypeStruct(x.shap...  1.91 us

profile of v7, /device:TPU:15, one launch (start us, length us, event | category | flops | bytes accessed | tf_op | source)
XLA Modules:
  0.0 39.4 jit_solution(13120030551144376097)
XLA Ops:
  0.6 36.8 %shard_map.59 = (f32[256,512]{1,0:T(8,128)}, f32[64,512]{1,0:T(8,128)}) custom-call(f32[256,512]{1,0:T(8,128)} %u_hbm.1, f32[128,512]{1,0:T(8,128)} %h_hbm.1, s32[4,8,256]{2,1,0:T(8,128)} %bitcast.2, s32[4,8,256]{2,1,0:T(8,128)} %bitcast.3), custom_call_target="tpu_custom_call" | custom-call | tf_op jit(solution)/shard_map/pallas_call | solution.py:339
  37.5 1.9 %shard_map.60 = (f32[256,512]{1,0:T(8,128)}, f32[64,512]{1,0:T(8,128)}) custom-call(f32[256,512]{1,0:T(8,128)} %get-tuple-element.4.u_in, f32[64,512]{1,0:T(8,128)} %get-tuple-element.5.i_in), custom_call_target="tpu_custom_call" | custom-call | tf_op jit(solution)/shard_map/pallas_call | solution.py:373

commit v8 on v5

--- a/solution.py
+++ b/solution.py
@@ -208,7 +208,7 @@
     for q in range(1, n_split):
         for p in range(PIECES):
             user_copies[n_split - q][p].wait_recv()
-            if paired and q == n_split - 1 and p == PIECES - 2:
+            if paired and q == n_split - 1 and p == PIECES // 2 - 1:
 
                 @pl.when(even)
                 def _():
@@ -304,9 +304,9 @@
 
 
 def store_kernel(u_in, i_in, u_out, i_out, u_buf, i_buf, load_sem, store_sem):
-    rows = u_in.shape[0] // PIECES
+    rows = u_in.shape[0] // PARTS
     pieces = [(i_in, i_buf, i_out)]
-    for p in range(PIECES):
+    for p in range(PARTS):
         at = pl.ds(p * rows, rows)
         pieces.append((u_in.at[at], u_buf.at[at], u_out.at[at]))
     loads = [
@@ -376,8 +376,8 @@
         out_specs=(pl.BlockSpec(memory_space=pl.ANY),) * 2,
         scratch_shapes=[
             *(pltpu.VMEM(x.shape, x.dtype) for x in results),
-            dma((PIECES + 1,)),
-            dma((PIECES + 1,)),
+            dma((PARTS + 1,)),
+            dma((PARTS + 1,)),
         ],
         compiler_params=pltpu.CompilerParams(vmem_limit_bytes=63 * 2**20),
     )(*results)

time: 36 us -> 35.3 us (0.981)
  the two profiles are of different devices: /device:TPU:1 before, /device:TPU:25 now
where the time goes in v8:
time: 35.3 us; the launch traced here: 35.1 us
  Pallas kernels  34.5 us (98%)
  between operations  0.64 us (2%)
    pallas_call x1, Pallas kernels, local(): pl.pallas_call(functools.partial(kernel, n_blk, n_split), out_shape=(jax....  32.6 us
    pallas_call x1, Pallas kernels, local(): pl.pallas_call(store_kernel, out_shape=tuple((jax.ShapeDtypeStruct(x.shap...  1.86 us

profile of v8, /device:TPU:25, one launch (start us, length us, event | category | flops | bytes accessed | tf_op | source)
XLA Modules:
  0.0 35.1 jit_solution(2569478955078862985)
XLA Ops:
  0.6 32.6 %shard_map.59 = (f32[256,512]{1,0:T(8,128)}, f32[64,512]{1,0:T(8,128)}) custom-call(f32[256,512]{1,0:T(8,128)} %u_hbm.1, f32[128,512]{1,0:T(8,128)} %h_hbm.1, s32[4,8,256]{2,1,0:T(8,128)} %bitcast.2, s32[4,8,256]{2,1,0:T(8,128)} %bitcast.3), custom_call_target="tpu_custom_call" | custom-call | tf_op jit(solution)/shard_map/pallas_call | solution.py:336
  33.3 1.9 %shard_map.60 = (f32[256,512]{1,0:T(8,128)}, f32[64,512]{1,0:T(8,128)}) custom-call(f32[256,512]{1,0:T(8,128)} %get-tuple-element.4.u_in, f32[64,512]{1,0:T(8,128)} %get-tuple-element.5.i_in), custom_call_target="tpu_custom_call" | custom-call | tf_op jit(solution)/shard_map/pallas_call | solution.py:372

commit v9 on v8

--- a/solution.py
+++ b/solution.py
@@ -208,7 +208,7 @@
     for q in range(1, n_split):
         for p in range(PIECES):
             user_copies[n_split - q][p].wait_recv()
-            if paired and q == n_split - 1 and p == PIECES // 2 - 1:
+            if paired and q == n_split - 1 and p == 0:
 
                 @pl.when(even)
                 def _():

time: 35.3 us -> 35.3 us (level)
  no operation moved by 1% of the time
where the time goes in v9:
time: 35.3 us; the launch traced here: 35.1 us
  Pallas kernels  34.5 us (98%)
  between operations  0.64 us (2%)
    pallas_call x1, Pallas kernels, local(): pl.pallas_call(functools.partial(kernel, n_blk, n_split), out_shape=(jax....  32.6 us
    pallas_call x1, Pallas kernels, local(): pl.pallas_call(store_kernel, out_shape=tuple((jax.ShapeDtypeStruct(x.shap...  1.86 us

profile of v9, /device:TPU:25, one launch (start us, length us, event | category | flops | bytes accessed | tf_op | source)
XLA Modules:
  0.0 35.1 jit_solution(3917283960992899097)
XLA Ops:
  0.6 32.6 %shard_map.59 = (f32[256,512]{1,0:T(8,128)}, f32[64,512]{1,0:T(8,128)}) custom-call(f32[256,512]{1,0:T(8,128)} %u_hbm.1, f32[128,512]{1,0:T(8,128)} %h_hbm.1, s32[4,8,256]{2,1,0:T(8,128)} %bitcast.2, s32[4,8,256]{2,1,0:T(8,128)} %bitcast.3), custom_call_target="tpu_custom_call" | custom-call | tf_op jit(solution)/shard_map/pallas_call | solution.py:336
  33.3 1.9 %shard_map.60 = (f32[256,512]{1,0:T(8,128)}, f32[64,512]{1,0:T(8,128)}) custom-call(f32[256,512]{1,0:T(8,128)} %get-tuple-element.4.u_in, f32[64,512]{1,0:T(8,128)} %get-tuple-element.5.i_in), custom_call_target="tpu_custom_call" | custom-call | tf_op jit(solution)/shard_map/pallas_call | solution.py:372
